TPU v7x, 32 devices: a whole 2x2x4 slice. The times are simulated.
32 devices in a mesh: store: 4 (over x, core), sku: 8 (over z, y).
Axes of the slice: x: 2, y: 2, z: 4, core: 2. Of those that a mesh axis runs over, the one named last changes fastest.
Arguments:
- base_bottom: float32 [32, 13, 4096], P(('store', 'sku')), may hold values from -6 to 6
- weight_bottom: float32 [32, 13, 4096], P(('store', 'sku')), may hold values from 0.5 to 4
- base_category: float32 [32, 13, 1024], P(('store', 'sku')), may hold values from -24 to 24
- weight_category: float32 [32, 13, 1024], P(('store', 'sku')), may hold values from 0.02 to 0.2
- base_region: float32 [32, 13, 4096], P(None, None, ('store', 'sku')), may hold values from -24 to 24
- weight_region: float32 [32, 13, 4096], P(None, None, ('store', 'sku')), may hold values from 0.02 to 0.2
- category_map: int32 [4096], replicated, may hold values from 0 to 1023
- region_map: int32 [32], replicated, may hold values from 0 to 31
Outputs:
- reconciled: float32 [32, 13, 4096], P(('store', 'sku'))
- residual: float32 [32, 13, 4096], P(('store', 'sku'))
All inputs are finite; a program needn't handle non-finite values.
Results may differ from a plain program's by a relative error of at most 0.0003.
Values sent between devices are 32-bit elements; how exact they have to be, the bound alone decides.
No kernel may reach another device: no remote copies, remote signals or barrier semaphores. Data moves between devices by JAX's collectives and lax.ppermute only.
A program may use at most 128 MiB of HBM per device.

v0:
```python
import math

import jax
import jax.numpy as jnp
from jax import lax
from jax.sharding import PartitionSpec as P

ITERS = 3


def table_times(table, values):
    return jnp.dot(
        table, values, precision=lax.Precision.HIGHEST, preferred_element_type=jnp.float32
    )


def category_sums(field, category_map, n_cat):
    stores, horizon, skus = field.shape
    rows = stores * horizon
    flat = field.reshape(rows, skus)
    width = math.gcd(skus, 2048)
    labels = jnp.arange(n_cat, dtype=jnp.int32)

    def accumulate(blocknum, total):
        start = blocknum * width
        columns = lax.dynamic_slice_in_dim(flat, start, width, 1)
        members = lax.dynamic_slice_in_dim(category_map, start, width, 0)
        onehot = (members[:, None] == labels[None, :]).astype(jnp.float32)
        return total + jnp.dot(
            columns, onehot, precision=lax.Precision.HIGHEST, preferred_element_type=jnp.float32
        )

    total = lax.fori_loop(0, skus // width, accumulate, jnp.zeros((rows, n_cat), jnp.float32))
    return total.reshape(stores, horizon, n_cat)


def category_spread(values, category_map, skus):
    stores, horizon, n_cat = values.shape
    rows = stores * horizon
    flat = values.reshape(rows, n_cat)
    width = math.gcd(skus, 2048)
    labels = jnp.arange(n_cat, dtype=jnp.int32)

    def place(blocknum, output):
        start = blocknum * width
        members = lax.dynamic_slice_in_dim(category_map, start, width, 0)
        onehot = (labels[:, None] == members[None, :]).astype(jnp.float32)
        block = jnp.dot(
            flat, onehot, precision=lax.Precision.HIGHEST, preferred_element_type=jnp.float32
        )
        return lax.dynamic_update_slice_in_dim(output, block, start, 1)

    output = lax.fori_loop(0, skus // width, place, jnp.zeros((rows, skus), jnp.float32))
    return output.reshape(stores, horizon, skus)


def to_region(field):
    return lax.all_to_all(field, ("store", "sku"), split_axis=2, concat_axis=0, tiled=True)


def from_region(field):
    return lax.all_to_all(field, ("store", "sku"), split_axis=0, concat_axis=2, tiled=True)


def squares(residual):
    return lax.psum(jnp.sum(residual * residual), ("store", "sku"))


def on_device(
    base_bottom,
    weight_bottom,
    base_category,
    weight_category,
    base_region,
    weight_region,
    category_map,
    region_map,
):
    n_cat = weight_category.shape[2]
    n_regions, horizon, sku_local = weight_region.shape
    skus = base_bottom.shape[2]
    all_stores = region_map.shape[0]
    region_ids = jnp.arange(n_regions, dtype=jnp.int32)
    gather_table = (region_ids[:, None] == region_map[None, :]).astype(jnp.float32)
    spread_table = (region_map[:, None] == region_ids[None, :]).astype(jnp.float32)

    def region_sums(field):
        moved = to_region(field).reshape(all_stores, horizon * sku_local)
        summed = table_times(gather_table, moved)
        return summed.reshape(n_regions, horizon, sku_local)

    def spread_both(cat_values, region_values):
        flat = region_values.reshape(n_regions, horizon * sku_local)
        spread = table_times(spread_table, flat)
        returned = from_region(spread.reshape(all_stores, horizon, sku_local))
        return category_spread(cat_values, category_map, skus) + returned

    reconciled = base_bottom
    region_start = weight_region * (base_region - region_sums(base_bottom))
    cat_start = weight_category * (base_category - category_sums(base_bottom, category_map, n_cat))
    residual = spread_both(cat_start, region_start)
    direction = residual
    norm_now = squares(residual)
    for repeat in range(ITERS):
        operate_region_values = weight_region * region_sums(direction)
        operate_cat_values = weight_category * category_sums(direction, category_map, n_cat)
        image = weight_bottom * direction + spread_both(operate_cat_values, operate_region_values)
        step_size = norm_now / lax.psum(jnp.sum(direction * image), ("store", "sku"))
        reconciled = reconciled + step_size * direction
        residual = residual - step_size * image
        norm_next = squares(residual)
        direction = residual + norm_next / norm_now * direction
        norm_now = norm_next
    return (reconciled, residual)


def solution(mesh):
    in_specs = (
        P(("store", "sku"), None, None),
        P(("store", "sku"), None, None),
        P(("store", "sku"), None, None),
        P(("store", "sku"), None, None),
        P(None, None, ("store", "sku")),
        P(None, None, ("store", "sku")),
        P(),
        P(),
    )
    out_specs = (P(("store", "sku"), None, None), P(("store", "sku"), None, None))
    return jax.shard_map(
        on_device, mesh=mesh, in_specs=in_specs, out_specs=out_specs, check_vma=False
    )
```

profile of v0, /device:TPU:0, one launch (start us, length us, event | category | flops | bytes accessed | tf_op | source)
XLA Modules:
  0.0 470.2 jit_solution(13211702110461980116)
XLA Ops:
  0.6 4.3 copy.131
  5.5 19.4 %reduce.2 = f32[4096,13]{1,0:T(8,128)} reduce(f32[4096,1,13]{2,1,0:T(1,128)S(1)} %bitcast.277, f32[]{:T(128)} %broadcast.52), dimensions={1}, to_apply=%bitcast.203.reduce_sub_computation | reduce | bytes 425988
  24.8 3.9 reshape.138
  28.7 7.8 %all-to-all-start = ((f32[32,1,1664]{2,1,0:T(1,128)}), f32[32,1,1664]{2,1,0:T(1,128)S(1)}, u32[]{:S(2)}, u32[]{:S(2)}) async-start(f32[32,1,1664]{2,1,0:T(1,128)} %reshape.138), calls=%async_computation | async-start | bytes 425984 | tf_op jit(solution)/shard_map/all_to_all | solution.py:58
  36.7 5.6 %while.116 = (s32[]{:T(128)}, f32[13,1024]{1,0:T(8,128)S(1)}, f32[13,4096]{1,0:T(8,128)S(1)}, s32[4096]{0:T(1024)S(1)}, s32[]{:T(128)}, /*index=5*/s32[]{:T(128)}, s32[]{:T(128)}, s32[]{:T(128)}) while((s32[]{:T(128)}, f32[13,1024]{1,0:T(8,128)S(1)}, f32[13,4096]{1,0:T(8,128)S(1)}, s32[4096]{0:T(1024)S(1)}, s32[]{:T(128)}, ...), condition=%wide.region_1.0_spmd.clone, body=%wide.region_0.0_spmd.clone.sunk | while | flops 329279488 | bytes 274581 | solution.py:33
  57.3 5.4 %while.112 = (s32[]{:T(128)}, f32[13,4096]{1,0:T(8,128)S(1)}, s32[4096]{0:T(1024)S(1)}, f32[13,1024]{1,0:T(8,128)S(1)}, s32[]{:T(128)}, /*index=5*/s32[]{:T(128)}, s32[]{:T(128)}, s32[]{:T(128)}) while((s32[]{:T(128)}, f32[13,4096]{1,0:T(8,128)S(1)}, s32[4096]{0:T(1024)S(1)}, f32[13,1024]{1,0:T(8,128)S(1)}, s32[]{:T(128)}, ...), condition=%wide.region_3.0_spmd.clone, body=%wide.region_2.0_spmd.clone.sunk | while | flops 329252864 | bytes 221323 | solution.py:53
  62.7 5.1 %all-to-all-done.1 = f32[32,13,128]{2,1,0:T(8,128)S(1)} async-done(((f32[32,13,128]{2,1,0:T(8,128)}), f32[32,13,128]{2,1,0:T(8,128)S(1)}, u32[]{:S(2)}, u32[]{:S(2)}) %all-to-all-start.1) | async-done | bytes 213024 | tf_op jit(solution)/shard_map/all_to_all | solution.py:62
  68.8 3.6 copy.141
  72.5 19.0 %reduce.4 = f32[4096,13]{1,0:T(8,128)S(1)} reduce(f32[4096,1,13]{2,1,0:T(1,128)} %bitcast.282, f32[]{:T(128)} %broadcast.52), dimensions={1}, to_apply=%bitcast.205.reduce_sub_computation | reduce | bytes 425988
  96.8 5.6 %while.117 = (s32[]{:T(128)}, f32[13,1024]{1,0:T(8,128)S(1)}, f32[13,4096]{1,0:T(8,128)S(1)}, s32[4096]{0:T(1024)S(1)}, s32[]{:T(128)}, /*index=5*/s32[]{:T(128)}, s32[]{:T(128)}, s32[]{:T(128)}) while((s32[]{:T(128)}, f32[13,1024]{1,0:T(8,128)S(1)}, f32[13,4096]{1,0:T(8,128)S(1)}, s32[4096]{0:T(1024)S(1)}, s32[]{:T(128)}, ...), condition=%wide.region_7.0_spmd.clone, body=%wide.region_6.0_spmd.clone.sunk | while | flops 329279488 | bytes 274581 | solution.py:33
  117.1 5.4 %while.113 = (s32[]{:T(128)}, f32[13,4096]{1,0:T(8,128)S(1)}, s32[4096]{0:T(1024)S(1)}, f32[13,1024]{1,0:T(8,128)S(1)}, s32[]{:T(128)}, /*index=5*/s32[]{:T(128)}, s32[]{:T(128)}, s32[]{:T(128)}) while((s32[]{:T(128)}, f32[13,4096]{1,0:T(8,128)S(1)}, s32[4096]{0:T(1024)S(1)}, f32[13,1024]{1,0:T(8,128)S(1)}, s32[]{:T(128)}, ...), condition=%wide.region_9.0_spmd.clone, body=%wide.region_8.0_spmd.clone.sunk | while | flops 329252864 | bytes 221323 | solution.py:53
  122.5 5.1 %all-to-all-done.3 = f32[32,13,128]{2,1,0:T(8,128)S(1)} async-done(((f32[32,13,128]{2,1,0:T(8,128)}), f32[32,13,128]{2,1,0:T(8,128)S(1)}, u32[]{:S(2)}, u32[]{:S(2)}) %all-to-all-start.3) | async-done | bytes 213024 | tf_op jit(solution)/shard_map/all_to_all | solution.py:62
  128.7 38.9 %all-reduce = (f32[]{:T(128)}, f32[]{:T(128)}) all-reduce(f32[]{:T(128)} %get-tuple-element.958, f32[]{:T(128)} %multiply_reduce_fusion.4), channel_id=1, replica_groups=mesh['store'=4,'sku'=8] {'store','sku'}, use_global_device_ids=true, to_apply=%region_5.0 | all-reduce | flops 2 | bytes 16 | tf_op jit(solution)/shard_map/psum | solution.py:66
  169.7 40.9 %psum.44 = f32[]{:T(128)} all-reduce(f32[]{:T(128)} %get-tuple-element.956), channel_id=1, replica_groups=mesh['store'=4,'sku'=8] {'store','sku'}, use_global_device_ids=true, to_apply=%region_13.0 | all-reduce | flops 1 | bytes 8 | tf_op jit(solution)/shard_map/psum | solution.py:66
  211.9 3.7 copy.152
  215.6 19.0 %reduce.6 = f32[4096,13]{1,0:T(8,128)S(1)} reduce(f32[4096,1,13]{2,1,0:T(1,128)} %bitcast.283, f32[]{:T(128)} %broadcast.52), dimensions={1}, to_apply=%bitcast.207.reduce_sub_computation | reduce | bytes 425988
  237.1 4.4 all-to-all-start.4
  241.5 5.6 %while.118 = (s32[]{:T(128)}, f32[13,1024]{1,0:T(8,128)S(1)}, f32[13,4096]{1,0:T(8,128)S(1)}, s32[4096]{0:T(1024)S(1)}, s32[]{:T(128)}, /*index=5*/s32[]{:T(128)}, s32[]{:T(128)}, s32[]{:T(128)}) while((s32[]{:T(128)}, f32[13,1024]{1,0:T(8,128)S(1)}, f32[13,4096]{1,0:T(8,128)S(1)}, s32[4096]{0:T(1024)S(1)}, s32[]{:T(128)}, ...), condition=%wide.region_15.0_spmd.clone, body=%wide.region_14.0_spmd.clone.sunk | while | flops 329279488 | bytes 274581 | solution.py:33
  264.2 5.4 %while.114 = (s32[]{:T(128)}, f32[13,4096]{1,0:T(8,128)S(1)}, s32[4096]{0:T(1024)S(1)}, f32[13,1024]{1,0:T(8,128)S(1)}, s32[]{:T(128)}, /*index=5*/s32[]{:T(128)}, s32[]{:T(128)}, s32[]{:T(128)}) while((s32[]{:T(128)}, f32[13,4096]{1,0:T(8,128)S(1)}, s32[4096]{0:T(1024)S(1)}, f32[13,1024]{1,0:T(8,128)S(1)}, s32[]{:T(128)}, ...), condition=%wide.region_17.0_spmd.clone, body=%wide.region_16.0_spmd.clone.sunk | while | flops 329252864 | bytes 221323 | solution.py:53
  269.6 5.2 %all-to-all-done.5 = f32[32,13,128]{2,1,0:T(8,128)S(1)} async-done(((f32[32,13,128]{2,1,0:T(8,128)}), f32[32,13,128]{2,1,0:T(8,128)S(1)}, u32[]{:S(2)}, u32[]{:S(2)}) %all-to-all-start.5) | async-done | bytes 213024 | tf_op jit(solution)/shard_map/all_to_all | solution.py:62
  275.8 38.8 %psum.45 = f32[]{:T(128)} all-reduce(f32[]{:T(128)} %multiply_reduce_fusion.2), channel_id=1, replica_groups=mesh['store'=4,'sku'=8] {'store','sku'}, use_global_device_ids=true, to_apply=%region_19.0 | all-reduce | flops 1 | bytes 8 | tf_op jit(solution)/shard_map/psum | solution.py:108
  316.8 40.7 %psum.46 = f32[]{:T(128)} all-reduce(f32[]{:T(128)} %get-tuple-element.954), channel_id=1, replica_groups=mesh['store'=4,'sku'=8] {'store','sku'}, use_global_device_ids=true, to_apply=%region_21.0 | all-reduce | flops 1 | bytes 8 | tf_op jit(solution)/shard_map/psum | solution.py:66
  358.8 3.7 copy.162
  362.5 19.0 %reduce.8 = f32[4096,13]{1,0:T(8,128)S(1)} reduce(f32[4096,1,13]{2,1,0:T(1,128)} %bitcast.284, f32[]{:T(128)} %broadcast.52), dimensions={1}, to_apply=%bitcast.209.reduce_sub_computation | reduce | bytes 425988
  384.0 4.5 all-to-all-start.6
  388.5 7.6 %while.119 = (s32[]{:T(128)}, f32[13,1024]{1,0:T(8,128)}, f32[13,4096]{1,0:T(8,128)S(1)}, s32[4096]{0:T(1024)S(1)}, s32[]{:T(128)}, /*index=5*/s32[]{:T(128)}, s32[]{:T(128)}, s32[]{:T(128)}) while((s32[]{:T(128)}, f32[13,1024]{1,0:T(8,128)}, f32[13,4096]{1,0:T(8,128)S(1)}, s32[4096]{0:T(1024)S(1)}, s32[]{:T(128)}, ...), condition=%wide.region_23.0_spmd.clone, body=%wide.region_22.0_spmd.clone.sunk | while | flops 329279488 | bytes 262293 | solution.py:33
  391.9 4.2 fusion.139
  399.5 4.2 reshape.145
  409.7 5.9 %all-to-all-start.7 = ((f32[32,13,128]{2,1,0:T(8,128)}), f32[32,13,128]{2,1,0:T(8,128)S(1)}, u32[]{:S(2)}, u32[]{:S(2)}) async-start(f32[32,13,128]{2,1,0:T(8,128)} %copy.168), calls=%async_computation.7 | async-start | bytes 524288 | tf_op jit(solution)/shard_map/all_to_all | solution.py:62
  415.7 5.4 %while.115 = (s32[]{:T(128)}, f32[13,4096]{1,0:T(8,128)S(1)}, s32[4096]{0:T(1024)S(1)}, f32[13,1024]{1,0:T(8,128)S(1)}, s32[]{:T(128)}, /*index=5*/s32[]{:T(128)}, s32[]{:T(128)}, s32[]{:T(128)}) while((s32[]{:T(128)}, f32[13,4096]{1,0:T(8,128)S(1)}, s32[4096]{0:T(1024)S(1)}, f32[13,1024]{1,0:T(8,128)S(1)}, s32[]{:T(128)}, ...), condition=%wide.region_25.0_spmd.clone, body=%wide.region_24.0_spmd.clone.sunk | while | flops 329252864 | bytes 221323 | solution.py:53
  421.2 5.2 %all-to-all-done.7 = f32[32,13,128]{2,1,0:T(8,128)S(1)} async-done(((f32[32,13,128]{2,1,0:T(8,128)}), f32[32,13,128]{2,1,0:T(8,128)S(1)}, u32[]{:S(2)}, u32[]{:S(2)}) %all-to-all-start.7) | async-done | bytes 213024 | tf_op jit(solution)/shard_map/all_to_all | solution.py:62
  427.4 38.8 %psum.47 = f32[]{:T(128)} all-reduce(f32[]{:T(128)} %multiply_reduce_fusion), channel_id=1, replica_groups=mesh['store'=4,'sku'=8] {'store','sku'}, use_global_device_ids=true, to_apply=%region_27.0 | all-reduce | flops 1 | bytes 8 | tf_op jit(solution)/shard_map/psum | solution.py:108
  (148 shorter events, 115.9 us)
Async XLA Ops:
  24.8 11.8 %copy-start.7 = (f32[1,13,4096]{2,0,1:T(1,128)S(1)}, f32[1,13,4096]{2,0,1:T(1,128)}, u32[]{:S(2)}) copy-start(f32[1,13,4096]{2,0,1:T(1,128)} %param.24) | copy-start | bytes 638980
  24.8 11.9 %copy-start.1 = (s32[4096]{0:T(1024)S(1)}, s32[4096]{0:T(1024)}, u32[]{:S(2)}) copy-start(s32[4096]{0:T(1024)} %param.30) | copy-start | bytes 49156
  28.7 16.9 %all-to-all-start = ((f32[32,1,1664]{2,1,0:T(1,128)}), f32[32,1,1664]{2,1,0:T(1,128)S(1)}, u32[]{:S(2)}, u32[]{:S(2)}) async-start(f32[32,1,1664]{2,1,0:T(1,128)} %reshape.138), calls=%async_computation | async-start | bytes 425984 | tf_op jit(solution)/shard_map/all_to_all | solution.py:58
  36.7 5.6 %copy-start.8 = (f32[1,13,1024]{2,0,1:T(1,128)S(1)}, f32[1,13,1024]{2,0,1:T(1,128)}, u32[]{:S(2)}) copy-start(f32[1,13,1024]{2,0,1:T(1,128)} %param.27) | copy-start | bytes 159748
  36.7 5.6 %copy-start.19 = (f32[1,13,1024]{2,0,1:T(1,128)S(1)}, f32[1,13,1024]{2,0,1:T(1,128)}, u32[]{:S(2)}) copy-start(f32[1,13,1024]{2,0,1:T(1,128)} %param.26) | copy-start | bytes 159748
  46.7 5.6 %copy-start.2 = (f32[32,13,128]{2,0,1:T(8,128)S(1)}, f32[32,13,128]{2,0,1:T(8,128)}, u32[]{:S(2)}) copy-start(f32[32,13,128]{2,0,1:T(8,128)} %param.29) | copy-start | bytes 638980
  46.7 5.6 %copy-start.12 = (f32[32,13,128]{2,0,1:T(8,128)S(1)}, f32[32,13,128]{2,0,1:T(8,128)}, u32[]{:S(2)}) copy-start(f32[32,13,128]{2,0,1:T(8,128)} %param.28) | copy-start | bytes 638980
  46.7 5.6 %copy-start.20 = (s32[32]{0:T(128)S(1)}, s32[32]{0:T(128)}, u32[]{:S(2)}) copy-start(s32[32]{0:T(128)} %param.31) | copy-start | bytes 388
  52.1 5.1 %copy-start.18 = (f32[13,1024]{1,0:T(8,128)S(1)}, f32[13,1024]{1,0:T(8,128)}, u32[]{:S(2)}) copy-start(f32[13,1024]{1,0:T(8,128)} %fusion.82) | copy-start | bytes 159748
  53.7 14.2 %all-to-all-start.1 = ((f32[32,13,128]{2,1,0:T(8,128)}), f32[32,13,128]{2,1,0:T(8,128)S(1)}, u32[]{:S(2)}, u32[]{:S(2)}) async-start(f32[32,13,128]{2,1,0:T(8,128)} %copy.137), calls=%async_computation.1 | async-start | bytes 524288 | tf_op jit(solution)/shard_map/all_to_all | solution.py:62
  91.5 5.2 %copy-start.14 = (f32[13,1024]{1,0:T(8,128)S(1)}, f32[13,1024]{1,0:T(8,128)}, u32[]{:S(2)}) copy-start(f32[13,1024]{1,0:T(8,128)} %custom-call.1) | copy-start | bytes 159748
  93.9 11.8 %all-to-all-start.2 = ((f32[32,1,1664]{2,1,0:T(1,128)}), f32[32,1,1664]{2,1,0:T(1,128)S(1)}, u32[]{:S(2)}, u32[]{:S(2)}) async-start(f32[32,1,1664]{2,1,0:T(1,128)} %reshape.140), calls=%async_computation.2 | async-start | bytes 425984 | tf_op jit(solution)/shard_map/all_to_all | solution.py:58
  96.8 5.6 %copy-start.9 = (f32[1,13,1024]{2,0,1:T(1,128)S(1)}, f32[1,13,1024]{2,0,1:T(1,128)}, u32[]{:S(2)}) copy-start(f32[1,13,1024]{2,0,1:T(1,128)} %param.27) | copy-start | bytes 159748
  112.3 4.8 %copy-start.16 = (f32[13,1024]{1,0:T(8,128)S(1)}, f32[13,1024]{1,0:T(8,128)}, u32[]{:S(2)}) copy-start(f32[13,1024]{1,0:T(8,128)} %fusion.83) | copy-start | bytes 159748
  113.9 13.8 %all-to-all-start.3 = ((f32[32,13,128]{2,1,0:T(8,128)}), f32[32,13,128]{2,1,0:T(8,128)S(1)}, u32[]{:S(2)}, u32[]{:S(2)}) async-start(f32[32,13,128]{2,1,0:T(8,128)} %copy.147), calls=%async_computation.3 | async-start | bytes 524288 | tf_op jit(solution)/shard_map/all_to_all | solution.py:62
  117.1 10.9 %copy-start = (f32[1,13,4096]{2,0,1:T(1,128)S(1)}, f32[1,13,4096]{2,0,1:T(1,128)}, u32[]{:S(2)}) copy-start(f32[1,13,4096]{2,0,1:T(1,128)} %param.25) | copy-start | bytes 638980
  169.7 45.9 %copy-start.5 = (f32[1,13,4096]{2,1,0:T(8,128)}, f32[1,13,4096]{2,1,0:T(8,128)S(1)}, u32[]{:S(2)}) copy-start(f32[1,13,4096]{2,1,0:T(8,128)S(1)} %get-tuple-element.957) | copy-start | bytes 638980
  234.7 6.8 %copy-start.13 = (f32[13,1024]{1,0:T(8,128)S(1)}, f32[13,1024]{1,0:T(8,128)}, u32[]{:S(2)}) copy-start(f32[13,1024]{1,0:T(8,128)} %custom-call.2) | copy-start | bytes 159748
  237.1 13.4 %all-to-all-start.4 = ((f32[32,1,1664]{2,1,0:T(1,128)}), f32[32,1,1664]{2,1,0:T(1,128)S(1)}, u32[]{:S(2)}, u32[]{:S(2)}) async-start(f32[32,1,1664]{2,1,0:T(1,128)} %reshape.142), calls=%async_computation.4 | async-start | bytes 425984 | tf_op jit(solution)/shard_map/all_to_all | solution.py:58
  241.5 5.6 %copy-start.10 = (f32[1,13,1024]{2,0,1:T(1,128)S(1)}, f32[1,13,1024]{2,0,1:T(1,128)}, u32[]{:S(2)}) copy-start(f32[1,13,1024]{2,0,1:T(1,128)} %param.27) | copy-start | bytes 159748
  258.5 5.7 %copy-start.17 = (f32[13,1024]{1,0:T(8,128)S(1)}, f32[13,1024]{1,0:T(8,128)}, u32[]{:S(2)}) copy-start(f32[13,1024]{1,0:T(8,128)} %fusion.84) | copy-start | bytes 159748
  261.0 13.8 %all-to-all-start.5 = ((f32[32,13,128]{2,1,0:T(8,128)}), f32[32,13,128]{2,1,0:T(8,128)S(1)}, u32[]{:S(2)}, u32[]{:S(2)}) async-start(f32[32,13,128]{2,1,0:T(8,128)} %copy.158), calls=%async_computation.5 | async-start | bytes 524288 | tf_op jit(solution)/shard_map/all_to_all | solution.py:62
  269.6 46.3 %copy-start.6 = (f32[1,13,4096]{2,1,0:T(8,128)S(1)}, f32[1,13,4096]{2,1,0:T(8,128)}, u32[]{:S(2)}) copy-start(f32[1,13,4096]{2,1,0:T(8,128)} %copy-done.5) | copy-start | bytes 638980
  316.8 45.8 %copy-start.3 = (f32[1,13,4096]{2,1,0:T(8,128)}, f32[1,13,4096]{2,1,0:T(8,128)S(1)}, u32[]{:S(2)}) copy-start(f32[1,13,4096]{2,1,0:T(8,128)S(1)} %get-tuple-element.955) | copy-start | bytes 638980
  384.0 13.7 %all-to-all-start.6 = ((f32[32,1,1664]{2,1,0:T(1,128)}), f32[32,1,1664]{2,1,0:T(1,128)S(1)}, u32[]{:S(2)}, u32[]{:S(2)}) async-start(f32[32,1,1664]{2,1,0:T(1,128)} %reshape.144), calls=%async_computation.6 | async-start | bytes 425984 | tf_op jit(solution)/shard_map/all_to_all | solution.py:58
  388.5 7.7 %copy-start.11 = (f32[1,13,1024]{2,0,1:T(1,128)S(1)}, f32[1,13,1024]{2,0,1:T(1,128)}, u32[]{:S(2)}) copy-start(f32[1,13,1024]{2,0,1:T(1,128)} %param.27) | copy-start | bytes 159748
  407.2 8.5 %copy-start.15 = (f32[13,1024]{1,0:T(8,128)S(1)}, f32[13,1024]{1,0:T(8,128)}, u32[]{:S(2)}) copy-start(f32[13,1024]{1,0:T(8,128)} %fusion.85) | copy-start | bytes 159748
  409.7 16.6 %all-to-all-start.7 = ((f32[32,13,128]{2,1,0:T(8,128)}), f32[32,13,128]{2,1,0:T(8,128)S(1)}, u32[]{:S(2)}, u32[]{:S(2)}) async-start(f32[32,13,128]{2,1,0:T(8,128)} %copy.168), calls=%async_computation.7 | async-start | bytes 524288 | tf_op jit(solution)/shard_map/all_to_all | solution.py:62
  421.2 46.4 %copy-start.4 = (f32[1,13,4096]{2,1,0:T(8,128)S(1)}, f32[1,13,4096]{2,1,0:T(8,128)}, u32[]{:S(2)}) copy-start(f32[1,13,4096]{2,1,0:T(8,128)} %copy-done.3) | copy-start | bytes 638980
where the time goes:
time: 477 us; the launch traced here: 470 us
  blocking collectives  198 us (42%)
  other arithmetic  90 us (19%)
  local copies, waits for them, and re-layouts  61.2 us (13%)
  matrix products  48.1 us (10%)
  starting transfers between devices  35.3 us (7%)
  waiting for transfers between devices  28.8 us (6%)
  between operations  8.38 us (2%)
    psum x3, blocking collectives, squares(): return lax.psum(jnp.sum(residual * residual), ('store', 'sku'))  121 us
    psum x2, blocking collectives, on_device(): lax.psum(jnp.sum(direction * image), ('store', 'sku'))  77.7 us
    unnamed x8, other arithmetic  76.5 us
    unnamed x63, local copies, waits for them, and re-layouts  32.8 us
    dot_general x8, matrix products, accumulate(): jnp.dot(columns, onehot, precision=lax.Precision.HIGHEST, preferred_eleme...  24.1 us
    dot_general x8, matrix products, place(): jnp.dot(flat, onehot, precision=lax.Precision.HIGHEST, preferred_element_...  21.6 us
    all_to_all x4, waiting for transfers between devices, from_region(): lax.all_to_all(field, ('store', 'sku'), split_axis=0, concat_axis=2, tile...  20.6 us
    all_to_all x4, starting transfers between devices, to_region(): lax.all_to_all(field, ('store', 'sku'), split_axis=2, concat_axis=0, tile...  19.5 us
  transfers between devices with their start and end apart: 8, of which 7 were waited for; matrix products, arithmetic and copies ran while one was open for 11% of the time, Pallas kernels for 0%

commit v1 on v0

v1 whole, which is shorter than its diff:
```python
import jax
import jax.numpy as jnp
from jax import lax
from jax.experimental import pallas as pl
from jax.experimental.pallas import tpu as pltpu
from jax.sharding import PartitionSpec as P

LANES = 128
PAD = 16
VMEM = pl.BlockSpec(memory_space=pltpu.VMEM)
SMEM = pl.BlockSpec(memory_space=pltpu.SMEM)


def exchange(blocks):
    return lax.all_to_all(blocks, ("store", "sku"), split_axis=0, concat_axis=0, tiled=True)


def call(body, outs, scratch, args, specs):
    return pl.pallas_call(
        body,
        out_shape=tuple(jax.ShapeDtypeStruct(shape, jnp.float32) for shape in outs),
        in_specs=specs,
        out_specs=tuple(VMEM for _ in outs),
        scratch_shapes=scratch,
        compiler_params=pltpu.CompilerParams(vmem_limit_bytes=40 << 20),
    )(*args)


def valid_rows(horizon):
    return lax.broadcasted_iota(jnp.int32, (PAD, LANES), 0) < horizon


def to_block(rows):
    horizon, lanes = rows.shape
    return jnp.concatenate([rows, jnp.zeros((PAD - horizon, lanes), rows.dtype)], axis=0)


def block_of(natural, j, horizon):
    return natural[0, :, pl.ds(pl.multiple_of(j * LANES, LANES), LANES)]


def category_sums(load, cat_ref, n_blocks, groups):
    width = 4 if n_blocks % 4 == 0 else 1
    lanes = width * LANES
    rows = groups * PAD

    def step(c, total):
        field = jnp.concatenate([load(c * width + i) for i in range(width)], axis=1)
        high = field.astype(jnp.bfloat16)
        low = (field - high.astype(jnp.float32)).astype(jnp.bfloat16)
        members = cat_ref[0:1, pl.ds(pl.multiple_of(c * lanes, LANES), lanes)]
        group = members // LANES
        labels = lax.broadcasted_iota(jnp.int32, (LANES, lanes), 0)
        table = jnp.where(labels == members % LANES, 1.0, 0.0).astype(jnp.bfloat16)
        group = jnp.broadcast_to(group, (PAD, lanes))
        masks = [jnp.where(group == g, 1.0, 0.0).astype(jnp.bfloat16) for g in range(groups)]
        spread = jnp.concatenate([high * m for m in masks] + [low * m for m in masks], axis=0)
        return total + lax.dot_general(
            spread, table, (((1,), (1,)), ((), ())), preferred_element_type=jnp.float32
        )

    total = lax.fori_loop(
        0, n_blocks // width, step, jnp.zeros((2 * rows, LANES), jnp.float32), unroll=2
    )
    return (total[:rows] + total[rows:]).reshape(groups, PAD, LANES)


def category_block(values, cat_ref, j, groups):
    members = cat_ref[0:1, pl.ds(pl.multiple_of(j * LANES, LANES), LANES)]
    members = jnp.broadcast_to(members, (PAD, LANES))
    place = members % LANES
    group = members // LANES
    result = jnp.zeros((PAD, LANES), jnp.float32)
    for g in range(groups):
        found = jnp.take_along_axis(values[g], place, axis=1)
        result = jnp.where(group == g, found, result)
    return result


def region_sums(load, map_ref, sums, n_blocks):
    sums[...] = jnp.zeros_like(sums)

    def step(s, carry):
        g = map_ref[s]
        sums[g] = sums[g] + load(s)
        return carry

    lax.fori_loop(0, n_blocks, step, 0, unroll=4)


def pack_body(base_ref, out_ref):
    n_blocks = out_ref.shape[0]
    horizon = base_ref.shape[1]

    def step(j, carry):
        out_ref[j] = to_block(block_of(base_ref, j, horizon))
        return carry

    lax.fori_loop(0, n_blocks, step, 0, unroll=4)


def category_start_body(
    base_ref, weight_ref, base_cat_ref, weight_cat_ref, cat_ref, spread_ref, diag_ref, wcat_ref
):
    n_blocks = spread_ref.shape[0]
    groups = wcat_ref.shape[0]
    horizon = weight_ref.shape[1]
    sums = category_sums(
        lambda j: to_block(block_of(base_ref, j, horizon)), cat_ref, n_blocks, groups
    )
    values = []
    for g in range(groups):
        lanes = slice(g * LANES, (g + 1) * LANES)
        weight = to_block(weight_cat_ref[0, :, lanes])
        wcat_ref[g] = weight
        values.append(weight * (to_block(base_cat_ref[0, :, lanes]) - sums[g]))

    def step(j, carry):
        diag_ref[j] = to_block(block_of(weight_ref, j, horizon))
        spread_ref[j] = category_block(values, cat_ref, j, groups)
        return carry

    lax.fori_loop(0, n_blocks, step, 0, unroll=2)


def region_start_body(moved_ref, base_ref, weight_ref, cat_part_ref, map_ref, send_ref, sums):
    n_blocks = moved_ref.shape[0]
    n_regions, horizon, _ = weight_ref.shape
    region_sums(lambda s: moved_ref[s], map_ref, sums, n_blocks)

    def scale(g, carry):
        weight = to_block(weight_ref[g])
        sums[g] = weight * (to_block(base_ref[g]) - sums[g])
        return carry

    lax.fori_loop(0, n_regions, scale, 0, unroll=4)

    def place(s, carry):
        send_ref[s, 0:PAD] = cat_part_ref[s]
        send_ref[s, PAD : 2 * PAD] = sums[map_ref[s]]
        return carry

    lax.fori_loop(0, n_blocks, place, 0, unroll=4)


def operate(r_ref, rs_ref, eps, diag_ref, wcat_ref, wreg_ref, cat_ref, map_ref, a_ref, q_ref, sums, merged):
    n_blocks = r_ref.shape[0]
    groups = wcat_ref.shape[0]
    n_regions, horizon, _ = wreg_ref.shape
    region_sums(lambda s: rs_ref[s], map_ref, sums, n_blocks)

    def scale(g, total):
        value = sums[g]
        scaled = to_block(wreg_ref[g]) * value
        sums[g] = scaled
        return total + scaled * value

    delta = lax.fori_loop(0, n_regions, scale, jnp.zeros((PAD, LANES), jnp.float32), unroll=4)

    cats = category_sums(lambda j: r_ref[j], cat_ref, n_blocks, groups)
    values = []
    for g in range(groups):
        scaled = wcat_ref[g] * cats[g]
        values.append(scaled)
        delta = delta + scaled * cats[g]

    def dots(j, carry):
        gamma, delta = carry
        r = r_ref[j]
        square = r * r
        return gamma + square, delta + diag_ref[j] * square

    gamma, delta = lax.fori_loop(
        0, n_blocks, dots, (jnp.zeros((PAD, LANES), jnp.float32), delta), unroll=4
    )
    line = lax.broadcasted_iota(jnp.int32, (PAD, LANES), 0)
    extra = jnp.zeros((PAD, LANES), jnp.float32)
    for i, part in enumerate((gamma, delta, eps)):
        extra = jnp.where(line == horizon + i, jnp.sum(part, axis=0, keepdims=True), extra)

    def place(j, carry):
        a = category_block(values, cat_ref, j, groups) + diag_ref[j] * r_ref[j]
        reg = sums[map_ref[j]]
        if merged:
            q_ref[j, 0:PAD] = a + extra
            q_ref[j, PAD : 2 * PAD] = reg
        else:
            a_ref[j] = a
            q_ref[j] = reg + extra
        return carry

    lax.fori_loop(0, n_blocks, place, 0, unroll=2)


def total_rows(load, n_blocks, horizon):
    total = lax.fori_loop(
        0,
        n_blocks,
        lambda j, total: total + load(j),
        jnp.zeros((PAD, LANES), jnp.float32),
        unroll=4,
    )
    sums = jnp.broadcast_to(jnp.sum(total, axis=1, keepdims=True), (PAD, LANES))
    return [
        jnp.broadcast_to(sums[horizon + i : horizon + i + 1], (PAD, LANES)) for i in range(3)
    ]


def first_body(
    sent_ref, got_ref, diag_ref, wcat_ref, wreg_ref, cat_ref, map_ref, r_ref, rs_ref, send_ref, sums
):
    n_blocks = r_ref.shape[0]

    def step(j, carry):
        r_ref[j] = sent_ref[j, 0:PAD] + got_ref[j, PAD : 2 * PAD]
        rs_ref[j] = got_ref[j, 0:PAD] + sent_ref[j, PAD : 2 * PAD]
        return carry

    lax.fori_loop(0, n_blocks, step, 0, unroll=4)
    operate(
        r_ref, rs_ref, jnp.zeros((PAD, LANES), jnp.float32), diag_ref, wcat_ref, wreg_ref,
        cat_ref, map_ref, None, send_ref, sums, True,
    )


def second_body(
    sent_ref, got_ref, x_ref, r_ref, rs_ref, diag_ref, wcat_ref, wreg_ref, cat_ref, map_ref,
    x_out, r_out, rs_out, s_out, ss_out, scal_ref, send_ref, sums,
):
    n_blocks = r_ref.shape[0]
    horizon = wreg_ref.shape[1]
    gamma, delta, _ = total_rows(lambda j: got_ref[j, 0:PAD], n_blocks, horizon)
    alpha = gamma / delta
    scal_ref[0] = gamma
    scal_ref[1] = delta
    valid = valid_rows(horizon)

    def step(j, eps):
        w = jnp.where(valid, sent_ref[j, 0:PAD] + got_ref[j, PAD : 2 * PAD], 0.0)
        ws = jnp.where(valid, got_ref[j, 0:PAD] + sent_ref[j, PAD : 2 * PAD], 0.0)
        r = r_ref[j]
        x_out[j] = x_ref[j] + alpha * r
        r = r - alpha * w
        r_out[j] = r
        s_out[j] = w
        rs_out[j] = rs_ref[j] - alpha * ws
        ss_out[j] = ws
        return eps + r * w

    eps = lax.fori_loop(0, n_blocks, step, jnp.zeros((PAD, LANES), jnp.float32), unroll=2)
    operate(
        r_out, rs_out, eps, diag_ref, wcat_ref, wreg_ref, cat_ref, map_ref, None, send_ref,
        sums, True,
    )


def third_body(
    sent_ref, got_ref, x_ref, r_ref, rs_ref, p_ref, s_ref, ss_ref, scal_ref,
    diag_ref, wcat_ref, wreg_ref, cat_ref, map_ref,
    x_out, r_out, p_out, s_out, scal_out, a_out, send_ref, sums, rs_out,
):
    n_blocks = r_ref.shape[0]
    horizon = wreg_ref.shape[1]
    gamma, delta, eps = total_rows(lambda j: got_ref[j, 0:PAD], n_blocks, horizon)
    beta = gamma / scal_ref[0]
    curve = delta + 2.0 * beta * eps + beta * beta * scal_ref[1]
    alpha = gamma / curve
    scal_out[0] = gamma
    scal_out[1] = curve
    valid = valid_rows(horizon)

    def step(j, eps):
        w = jnp.where(valid, sent_ref[j, 0:PAD] + got_ref[j, PAD : 2 * PAD], 0.0)
        ws = jnp.where(valid, got_ref[j, 0:PAD] + sent_ref[j, PAD : 2 * PAD], 0.0)
        s = w + beta * s_ref[j]
        r = r_ref[j]
        p = r + beta * p_ref[j]
        x_out[j] = x_ref[j] + alpha * p
        r = r - alpha * s
        r_out[j] = r
        p_out[j] = p
        s_out[j] = s
        rs_out[j] = rs_ref[j] - alpha * (ws + beta * ss_ref[j])
        return eps + r * s

    eps = lax.fori_loop(0, n_blocks, step, jnp.zeros((PAD, LANES), jnp.float32), unroll=2)
    operate(
        r_out, rs_out, eps, diag_ref, wcat_ref, wreg_ref, cat_ref, map_ref, a_out, send_ref,
        sums, False,
    )


def last_body(a_ref, got_ref, x_ref, r_ref, p_ref, s_ref, scal_ref, x_out, r_out):
    n_blocks = r_ref.shape[0]
    horizon = x_out.shape[1]
    gamma, delta, eps = total_rows(lambda j: got_ref[j], n_blocks, horizon)
    beta = gamma / scal_ref[0]
    alpha = gamma / (delta + 2.0 * beta * eps + beta * beta * scal_ref[1])

    def step(j, carry):
        r = r_ref[j]
        s = a_ref[j] + got_ref[j] + beta * s_ref[j]
        p = r + beta * p_ref[j]
        lanes = pl.ds(pl.multiple_of(j * LANES, LANES), LANES)
        x_out[0, :, lanes] = (x_ref[j] + alpha * p)[:horizon]
        r_out[0, :, lanes] = (r - alpha * s)[:horizon]
        return carry

    lax.fori_loop(0, n_blocks, step, 0, unroll=2)


def on_device(
    base_bottom,
    weight_bottom,
    base_category,
    weight_category,
    base_region,
    weight_region,
    category_map,
    region_map,
):
    n_cat = weight_category.shape[2]
    n_regions = weight_region.shape[0]
    n_blocks = region_map.shape[0]
    groups = n_cat // LANES
    cats = category_map.reshape(1, -1)
    blocks = (n_blocks, PAD, LANES)
    double = (n_blocks, 2 * PAD, LANES)
    sums = pltpu.VMEM((n_regions, PAD, LANES), jnp.float32)
    scal = (2, PAD, LANES)

    (x,) = call(pack_body, [blocks], [], (base_bottom,), [VMEM])
    moved = exchange(x)
    cat_part, diag, wcat = call(
        category_start_body,
        [blocks, blocks, (groups, PAD, LANES)],
        [],
        (base_bottom, weight_bottom, base_category, weight_category, cats),
        [VMEM] * 5,
    )
    (sent,) = call(
        region_start_body,
        [double],
        [sums],
        (moved, base_region, weight_region, cat_part, region_map),
        [VMEM] * 4 + [SMEM],
    )
    got = exchange(sent)
    fixed = (diag, wcat, weight_region, cats, region_map)
    fixed_specs = [VMEM] * 4 + [SMEM]
    r, rs, sent = call(
        first_body, [blocks, blocks, double], [sums], (sent, got) + fixed, [VMEM] * 2 + fixed_specs
    )
    got = exchange(sent)
    p = r
    x, r, rs, s, ss, scalars, sent = call(
        second_body,
        [blocks] * 5 + [scal, double],
        [sums],
        (sent, got, x, r, rs) + fixed,
        [VMEM] * 5 + fixed_specs,
    )
    got = exchange(sent)
    x, r, p, s, scalars, a, sent = call(
        third_body,
        [blocks] * 4 + [scal, blocks, blocks],
        [sums, pltpu.VMEM(blocks, jnp.float32)],
        (sent, got, x, r, rs, p, s, ss, scalars) + fixed,
        [VMEM] * 9 + fixed_specs,
    )
    got = exchange(sent)
    return call(
        last_body,
        [base_bottom.shape, base_bottom.shape],
        [],
        (a, got, x, r, p, s, scalars),
        [VMEM] * 7,
    )


def solution(mesh):
    in_specs = (
        P(("store", "sku"), None, None),
        P(("store", "sku"), None, None),
        P(("store", "sku"), None, None),
        P(("store", "sku"), None, None),
        P(None, None, ("store", "sku")),
        P(None, None, ("store", "sku")),
        P(),
        P(),
    )
    out_specs = (P(("store", "sku"), None, None), P(("store", "sku"), None, None))
    return jax.shard_map(
        on_device, mesh=mesh, in_specs=in_specs, out_specs=out_specs, check_vma=False
    )
```

time: 477 us -> 106 us (0.22); the launches traced: 470 us -> 105 us
  blocking collectives: 198 us -> 68.4 us
  other arithmetic: 90 us -> 0 us
  local copies, waits for them, and re-layouts: 61.2 us -> 6.35 us
  matrix products: 48.1 us -> 0 us
  starting transfers between devices: 35.3 us -> 7.3 us
  waiting for transfers between devices: 28.8 us -> 3.81 us
  Pallas kernels: 0 us -> 18.7 us
  between operations: 8.38 us -> 0.74 us
    psum x5 -> x0, blocking collectives: 198 us -> none  [the longest x3 121 us: squares(): return lax.psum(jnp.sum(residual * residual), ('store', 'sku'))]
    unnamed x8 -> x0, other arithmetic: 76.5 us -> none
    all_to_all x0 -> x4, blocking collectives: none -> 68.4 us  [exchange(): lax.all_to_all(blocks, ('store', 'sku'), split_axis=0, concat_axis=0, til...]
    dot_general x24 -> x0, matrix products: 48.1 us -> none  [the longest x8 24.1 us: accumulate(): jnp.dot(columns, onehot, precision=lax.Precision.HIGHEST, preferred_eleme...]
    unnamed x63 -> x20, local copies, waits for them, and re-layouts: 32.8 us -> 4.55 us
    all_to_all x8 -> x1, starting transfers between devices: 35.3 us -> 7.3 us  [exchange(): lax.all_to_all(blocks, ('store', 'sku'), split_axis=0, concat_axis=0, til...]
    all_to_all x8 -> x1, waiting for transfers between devices: 28.8 us -> 3.81 us  [exchange(): lax.all_to_all(blocks, ('store', 'sku'), split_axis=0, concat_axis=0, til...]
    pallas_call x0 -> x7, Pallas kernels: none -> 18.7 us  [call(): pl.pallas_call(body, out_shape=tuple((jax.ShapeDtypeStruct(shape, jnp.flo...]
  transfers between devices with their start and end apart: 8 -> 1, of which waited for: 7 -> 1; matrix products, arithmetic and copies ran while one was open for 11% -> 0% of each run, Pallas kernels for 0% -> 3%
where the time goes in v1:
time: 106 us; the launch traced here: 105 us
  blocking collectives  68.4 us (65%)
  Pallas kernels  18.7 us (18%)
  starting transfers between devices  7.3 us (7%)
  local copies, waits for them, and re-layouts  6.35 us (6%)
  waiting for transfers between devices  3.81 us (4%)
    all_to_all x4, blocking collectives, exchange(): lax.all_to_all(blocks, ('store', 'sku'), split_axis=0, concat_axis=0, til...  68.4 us
    pallas_call x7, Pallas kernels, call(): pl.pallas_call(body, out_shape=tuple((jax.ShapeDtypeStruct(shape, jnp.flo...  18.7 us
    all_to_all x1, starting transfers between devices, exchange(): lax.all_to_all(blocks, ('store', 'sku'), split_axis=0, concat_axis=0, til...  7.3 us
    unnamed x20, local copies, waits for them, and re-layouts  4.55 us
    all_to_all x1, waiting for transfers between devices, exchange(): lax.all_to_all(blocks, ('store', 'sku'), split_axis=0, concat_axis=0, til...  3.81 us
  transfers between devices with their start and end apart: 1, of which 1 were waited for; matrix products, arithmetic and copies ran while one was open for 0% of the time, Pallas kernels for 3%

profile of v1, /device:TPU:0, one launch (start us, length us, event | category | flops | bytes accessed | tf_op | source)
XLA Modules:
  0.0 105.3 jit_solution(5737606859113451722)
XLA Ops:
  0.6 1.1 %copy.10.base_ref = f32[1,13,4096]{2,1,0:T(8,128)S(1)} copy(f32[1,13,4096]{2,0,1:T(1,128)} %param.8) | data formatting | bytes 425984 | tf_op args[0]
  1.7 0.8 shard_map.95.x_ref
  2.5 0.0 copy-start.6
  2.5 7.3 %all-to-all-start = ((f32[32,16,128]{2,1,0:T(8,128)}), f32[32,16,128]{2,1,0:T(8,128)S(1)}, u32[]{:S(2)}, u32[]{:S(2)}) async-start(f32[32,16,128]{2,1,0:T(8,128)} %shard_map.95.x_ref), calls=%async_computation | async-start | bytes 524288 | tf_op jit(solution)/shard_map/all_to_all | solution.py:15
  9.8 0.0 copy-done.5
  9.8 0.0 copy-start.2
  9.8 0.0 copy-done.6
  9.8 0.9 copy-done.2
  10.7 0.0 copy-start.3
  10.7 0.1 copy.16.weight_ref.wreg_ref
  10.8 0.8 copy-done.3
  11.6 0.0 copy-start.4
  11.7 0.1 copy.12.weight_ref
  11.8 0.8 copy-done.4
  12.6 0.0 copy-start
  12.6 0.1 copy.15.base_ref
  12.7 0.6 copy-done
  13.3 3.3 %shard_map.96 = (f32[32,16,128]{2,1,0:T(8,128)S(1)}, f32[32,16,128]{2,1,0:T(8,128)S(1)}, f32[8,16,128]{2,1,0:T(8,128)S(1)}) custom-call(f32[1,13,4096]{2,1,0:T(8,128)S(1)} %copy.10.base_ref, f32[1,13,4096]{2,1,0:T(8,128)S(1)} %copy.12.weight_ref, f32[1,13,1024]{2,1,0:T(8,128)S(1)} %copy.13.base_cat_ref, f32[1,13,1024]{2,1,0:T(8,128)S(1)} %copy.14.weight_cat_ref, ...), custom_call_target="tpu_custom_call" | custom-call | tf_op jit(solution)/shard_map/pallas_call | solution.py:19
  16.6 0.0 copy-start.1
  16.6 3.8 %all-to-all-done.moved_ref = f32[32,16,128]{2,1,0:T(8,128)S(1)} async-done(((f32[32,16,128]{2,1,0:T(8,128)}), f32[32,16,128]{2,1,0:T(8,128)S(1)}, u32[]{:S(2)}, u32[]{:S(2)}) %all-to-all-start) | async-done | bytes 262176 | tf_op jit(solution)/shard_map/all_to_all | solution.py:15
  20.4 0.0 copy-done.1
  20.4 0.8 shard_map.97.sent_ref
  21.2 18.8 %all_to_all.25.got_ref = f32[32,32,128]{2,1,0:T(8,128)S(1)} all-to-all(f32[32,32,128]{2,1,0:T(8,128)S(1)} %shard_map.97.sent_ref), channel_id=1, replica_groups=mesh['store'=4,'sku'=8] {'store','sku'}, dimensions={0} | all-to-all | bytes 1048576 | tf_op jit(solution)/shard_map/all_to_all | solution.py:15
  40.1 4.2 %shard_map.98 = (f32[32,16,128]{2,1,0:T(8,128)S(1)}, f32[32,16,128]{2,1,0:T(8,128)S(1)}, f32[32,32,128]{2,1,0:T(8,128)S(1)}) custom-call(f32[32,32,128]{2,1,0:T(8,128)S(1)} %shard_map.97.sent_ref, f32[32,32,128]{2,1,0:T(8,128)S(1)} %all_to_all.25.got_ref, f32[32,16,128]{2,1,0:T(8,128)S(1)} %get-tuple-element.23.diag_ref, ...), custom_call_target="tpu_custom_call" | custom-call | tf_op jit(solution)/shard_map/pallas_call | solution.py:19
  44.2 18.4 %all_to_all.26.got_ref = f32[32,32,128]{2,1,0:T(8,128)S(1)} all-to-all(f32[32,32,128]{2,1,0:T(8,128)S(1)} %get-tuple-element.25.sent_ref), channel_id=1, replica_groups=mesh['store'=4,'sku'=8] {'store','sku'}, dimensions={0} | all-to-all | bytes 1048576 | tf_op jit(solution)/shard_map/all_to_all | solution.py:15
  62.6 4.8 %shard_map.99 = (f32[32,16,128]{2,1,0:T(8,128)S(1)}, f32[32,16,128]{2,1,0:T(8,128)S(1)}, f32[32,16,128]{2,1,0:T(8,128)S(1)}, f32[32,16,128]{2,1,0:T(8,128)S(1)},...) custom-call(f32[32,32,128]{2,1,0:T(8,128)S(1)} %get-tuple-element.25.sent_ref, ...), custom_call_target="tpu_custom_call" | custom-call | tf_op jit(solution)/shard_map/pallas_call | solution.py:19
  67.5 18.4 %all_to_all.27.got_ref = f32[32,32,128]{2,1,0:T(8,128)S(1)} all-to-all(f32[32,32,128]{2,1,0:T(8,128)S(1)} %get-tuple-element.28.sent_ref), channel_id=1, replica_groups=mesh['store'=4,'sku'=8] {'store','sku'}, dimensions={0} | all-to-all | bytes 1048576 | tf_op jit(solution)/shard_map/all_to_all | solution.py:15
  85.9 4.6 %shard_map.100 = (f32[32,16,128]{2,1,0:T(8,128)S(1)}, f32[32,16,128]{2,1,0:T(8,128)S(1)}, f32[32,16,128]{2,1,0:T(8,128)S(1)}, f32[32,16,128]{2,1,0:T(8,128)S(1)}...) custom-call(f32[32,32,128]{2,1,0:T(8,128)S(1)} %get-tuple-element.28.sent_ref, ...), custom_call_target="tpu_custom_call" | custom-call | tf_op jit(solution)/shard_map/pallas_call | solution.py:19
  90.5 12.7 %all_to_all.28.got_ref = f32[32,16,128]{2,1,0:T(8,128)S(1)} all-to-all(f32[32,16,128]{2,1,0:T(8,128)S(1)} %get-tuple-element.36), channel_id=1, replica_groups=mesh['store'=4,'sku'=8] {'store','sku'}, dimensions={0} | all-to-all | bytes 524288 | tf_op jit(solution)/shard_map/all_to_all | solution.py:15
  103.2 0.3 shard_map.101
  103.5 0.9 copy.20
  104.4 0.9 copy.21
  (3 shorter events, 0.0 us)
Async XLA Ops:
  2.5 7.3 %copy-start.5 = (f32[1,13,1024]{2,0,1:T(1,128)S(1)}, f32[1,13,1024]{2,0,1:T(1,128)}, u32[]{:S(2)}) copy-start(f32[1,13,1024]{2,0,1:T(1,128)} %param.10) | copy-start | bytes 159748
  2.5 7.4 %copy-start.6 = (f32[1,13,1024]{2,0,1:T(1,128)S(1)}, f32[1,13,1024]{2,0,1:T(1,128)}, u32[]{:S(2)}) copy-start(f32[1,13,1024]{2,0,1:T(1,128)} %param.11) | copy-start | bytes 159748
  2.5 18.0 %all-to-all-start = ((f32[32,16,128]{2,1,0:T(8,128)}), f32[32,16,128]{2,1,0:T(8,128)S(1)}, u32[]{:S(2)}, u32[]{:S(2)}) async-start(f32[32,16,128]{2,1,0:T(8,128)} %shard_map.95.x_ref), calls=%async_computation | async-start | bytes 524288 | tf_op jit(solution)/shard_map/all_to_all | solution.py:15
  9.8 0.9 copy-start.2
  10.7 0.9 copy-start.3
  11.6 0.9 copy-start.4
  12.6 0.7 copy-start
  16.6 3.8 %copy-start.1 = (s32[32]{0:T(128)S(1)}, s32[32]{0:T(128)}, u32[]{:S(2)}) copy-start(s32[32]{0:T(128)} %map_ref.7) | copy-start | bytes 388
